TPU v7x, 256 devices: a whole 4x4x8 slice. The times are simulated.
256 devices in a mesh: row: 16 (over y, z_lo, core), col: 16 (over x, z_hi).
Axes of the slice: x: 4, y: 4, z: 8 (z_hi: 4, z_lo: 2; z = z_hi * 2 + z_lo), core: 2. Of those that a mesh axis runs over, the one named last changes fastest.
Arguments:
- strips: bfloat16 [16, 16, 4, 1, 2048, 128], P('row', 'col'), may hold values from -6 to 6
- occupancy: int32 [16, 16], replicated, may hold values 0 or 1
Outputs:
- correlations: float32 [16, 16, 8, 128, 128], P('row', 'col')
All inputs are finite; a program needn't handle non-finite values.
Results may differ from a plain program's by a relative error of at most 0.0094.
Values may be sent and summed in bfloat16 or wider, within the bound.
A program may use at most 128 MiB of HBM per device.

v0:
```python
import math

import jax
import jax.numpy as jnp
from jax import lax
from jax.sharding import PartitionSpec as P


def from_behind(value, axis, steps):
    count = lax.axis_size(axis)
    initial, last = (max(0, -steps), min(count, count - steps))
    return lax.ppermute(value, axis, [(source, source + steps) for source in range(initial, last)])


def table_rows(row_index, length):
    column = lax.iota(jnp.int32, length)
    product = row_index[:, None] * column[None, :] % length
    angle = product.astype(jnp.float32) * (2.0 * math.pi / length)
    return (jnp.cos(angle).astype(jnp.bfloat16), jnp.sin(angle).astype(jnp.bfloat16))


def spin_matrix(breadth, forward):
    cosine, sine_table = table_rows(lax.iota(jnp.int32, breadth), breadth)
    upper_right = -sine_table if forward else sine_table
    return jnp.concatenate(
        [jnp.concatenate([cosine, upper_right], 1), jnp.concatenate([-upper_right, cosine], 1)], 0
    )


def along_length(flattened, length, row_block):
    real_parts = []
    imag_parts = []
    for first_row in range(0, length, row_block):
        cosine, sine_table = table_rows(lax.iota(jnp.int32, row_block) + first_row, length)
        real_parts.append(jnp.dot(cosine, flattened, preferred_element_type=jnp.float32))
        imag_parts.append(-jnp.dot(sine_table, flattened, preferred_element_type=jnp.float32))
    return (
        jnp.concatenate(real_parts, 0).astype(jnp.bfloat16),
        jnp.concatenate(imag_parts, 0).astype(jnp.bfloat16),
    )


def transform(pieces, row_block):
    planes, length, breadth = pieces[0].shape
    joined = jnp.concatenate(pieces, 0)
    pieces_count = joined.shape[0]
    flattened = jnp.transpose(joined, (1, 0, 2)).reshape(length, pieces_count * breadth)
    real_part, imag_part = along_length(flattened, length, row_block)
    halves = jnp.concatenate(
        [
            real_part.reshape(length, pieces_count, breadth),
            imag_part.reshape(length, pieces_count, breadth),
        ],
        2,
    )
    spectrum = jnp.einsum(
        "nqc,cd->nqd", halves, spin_matrix(breadth, True), preferred_element_type=jnp.float32
    ).astype(jnp.bfloat16)
    return [spectrum[:, k * planes : (k + 1) * planes] for k in range(len(pieces))]


def correlate(left_spec, right_spec, row_index):
    length, planes, doubled = left_spec.shape
    breadth = doubled // 2
    left_full = left_spec.astype(jnp.float32)
    right_full = right_spec.astype(jnp.float32)
    real_left, imag_left = (left_full[..., :breadth], left_full[..., breadth:])
    real_right, imag_right = (right_full[..., :breadth], right_full[..., breadth:])
    cross_real = real_left * real_right + imag_left * imag_right
    cross_imag = imag_left * real_right - real_left * imag_right
    magnitude = jnp.sqrt(cross_real * cross_real + cross_imag * cross_imag)
    lower_bound = 0.5 * jnp.mean(magnitude, axis=(0, 2), keepdims=True) + 1e-06
    inverse_size = 1.0 / jnp.maximum(magnitude, lower_bound)
    summed = jnp.concatenate(
        [jnp.sum(cross_real * inverse_size, axis=1), jnp.sum(cross_imag * inverse_size, axis=1)], 1
    ).astype(jnp.bfloat16)
    partial_back = jnp.dot(
        summed, spin_matrix(breadth, False), preferred_element_type=jnp.float32
    ).astype(jnp.bfloat16)
    cosine, sine_table = table_rows(row_index, length)
    weights = jnp.concatenate([cosine, -sine_table], 1)
    stacked = jnp.concatenate([partial_back[:, :breadth], partial_back[:, breadth:]], 0)
    return jnp.dot(weights, stacked, preferred_element_type=jnp.float32) / (
        planes * math.sqrt(length * breadth)
    )


def per_device(strips, occupancy):
    planes, length, breadth = strips.shape[3:]
    row_block = min(length, 512)
    local_strips = strips[0, 0]
    east_strip = local_strips[0]
    west_strip = local_strips[1]
    south_strip = local_strips[2]
    north_strip = local_strips[3]
    row_place = lax.axis_index("row")
    col_place = lax.axis_index("col")
    padded = jnp.pad(occupancy, 1)
    beside_all = lax.dynamic_slice(padded, (row_place, col_place), (3, 3)).astype(jnp.float32)
    live_east = beside_all[1, 1] * beside_all[1, 2]
    live_south = beside_all[1, 1] * beside_all[2, 1]
    live_right_down = beside_all[1, 1] * beside_all[2, 2]
    live_left_down = beside_all[1, 1] * beside_all[2, 0]
    live_left_up = beside_all[0, 0] * beside_all[1, 1]
    live_right_up = beside_all[0, 2] * beside_all[1, 1]
    edge_rows = (lax.iota(jnp.int32, breadth) - breadth // 2) % length
    corner_rows = lax.iota(jnp.int32, breadth)
    zero_map = jnp.zeros((breadth, breadth), jnp.float32)
    corner_top_left = west_strip[:, :breadth]
    corner_top_right = east_strip[:, :breadth]
    corner_low_right = east_strip[:, length - breadth :]
    corner_low_left = west_strip[:, length - breadth :]
    sent_west, sent_north = (west_strip, north_strip)
    from_below = from_behind((sent_north, corner_top_left, corner_top_right), "row", -1)
    from_above = from_behind((corner_low_right, corner_low_left), "row", 1)
    from_right = from_behind((sent_west, from_below[1], from_above[1]), "col", -1)
    from_left = from_behind((from_below[2], from_above[0]), "col", 1)
    owned = (east_strip, south_strip)
    partners = (from_right[0], from_below[0])

    def edge_maps(chosen):
        all_spectra = transform(
            [owned[k] for k in chosen] + [partners[k] for k in chosen], row_block
        )
        own_spectra = all_spectra[: len(chosen)]
        partner_spectra = all_spectra[len(chosen) :]
        return tuple(
            (correlate(own_spectra[k], partner_spectra[k], edge_rows) for k in range(len(chosen)))
        )

    east_map = lax.cond(live_east > 0, lambda: edge_maps((0,))[0], lambda: zero_map)
    south_map = lax.cond(live_south > 0, lambda: edge_maps((1,))[0], lambda: zero_map)
    east_map = east_map * live_east
    south_map = south_map * live_south
    corner_spectra = transform(
        [
            corner_low_right,
            from_right[1],
            corner_low_left,
            from_left[0],
            from_left[1],
            corner_top_left,
            from_right[2],
            corner_top_right,
        ],
        breadth,
    )
    right_down_map = correlate(corner_spectra[0], corner_spectra[1], corner_rows) * live_right_down
    left_down_map = correlate(corner_spectra[2], corner_spectra[3], corner_rows) * live_left_down
    left_up_map = correlate(corner_spectra[4], corner_spectra[5], corner_rows) * live_left_up
    right_up_map = correlate(corner_spectra[6], corner_spectra[7], corner_rows) * live_right_up
    from_west = from_behind(east_map.astype(jnp.bfloat16), "col", 1).astype(east_map.dtype)
    from_north = from_behind(south_map.astype(jnp.bfloat16), "row", 1).astype(south_map.dtype)
    result = jnp.stack(
        [
            east_map,
            south_map,
            right_down_map,
            left_down_map,
            from_west,
            from_north,
            left_up_map,
            right_up_map,
        ],
        0,
    )
    return result[None, None]


def solution(mesh):
    in_specs = (P("row", "col", None, None, None, None), P())
    out_specs = P("row", "col", None, None, None)
    return jax.shard_map(
        per_device, mesh=mesh, in_specs=in_specs, out_specs=out_specs, check_vma=False
    )
```

profile of v0, /device:TPU:54, one launch (start us, length us, event | category | flops | bytes accessed | tf_op | source)
XLA Modules:
  0.0 396.8 jit_solution(10554819870397265685)
XLA Ops:
  0.0 1.5 fusion.422
  1.7 7.6 %collective-permute-start = (bf16[1,2048,128]{1,2,0:T(8,128)(2,1)S(1)}, bf16[1,2048,128]{1,2,0:T(8,128)(2,1)S(1)}, u32[]{:S(2)}, u32[]{:S(2)}) collective-permute-start(bf16[1,2048,128]{1,2,0:T(8,128)(2,1)S(1)} %bitcast.179), channel_id=1, source_target_pairs={{1,0},{2,1},{3,2},{4,3},{5,4},{6,5},{7,6},{8,7},{9,8},{10,9},{11,1... | collective-permute-start | bytes 1572872 | tf_op jit(solution)/shard_map/ppermute | solution.py:12
  9.3 2.1 collective-permute-start.2
  11.6 2.9 collective-permute-start.4
  14.5 1.9 collective-permute-start.6
  17.4 3.6 collective-permute-start.1
  21.9 9.7 %collective-permute-done.2 = bf16[1,128,128]{1,2,0:T(8,128)(2,1)S(1)} collective-permute-done((bf16[1,128,128]{1,2,0:T(8,128)(2,1)S(1)}, bf16[1,128,128]{1,2,0:T(8,128)(2,1)S(1)}, u32[]{:S(2)}, u32[]{:S(2)}) %collective-permute-start.2) | collective-permute-done | bytes 32800 | tf_op jit(solution)/shard_map/ppermute | solution.py:12
  31.6 4.0 %collective-permute-start.3 = (bf16[1,128,128]{1,2,0:T(8,128)(2,1)S(1)}, bf16[1,128,128]{1,2,0:T(8,128)(2,1)S(1)}, u32[]{:S(2)}, u32[]{:S(2)}) collective-permute-start(bf16[1,128,128]{1,2,0:T(8,128)(2,1)S(1)} %collective-permute-done.2), channel_id=1, source_target_pairs={{1,0},{2,1},{3,2},{4,3},{5,4},{6,5},{7,6},{8,7},{9,8},{10,9},{11,1... | collective-permute-start | bytes 98312 | tf_op jit(solution)/shard_map/ppermute | solution.py:12
  35.7 2.7 collective-permute-start.5
  38.4 2.3 collective-permute-start.7
  40.8 3.7 collective-permute-done.5
  44.5 3.1 collective-permute-done.7
  47.6 1.9 collective-permute-start.8
  50.2 2.6 collective-permute-done.8
  52.9 3.7 collective-permute-start.9
  74.2 156.0 %conditional.2 = (f32[128,128]{1,0:T(8,128)S(1)}) conditional(s32[]{:T(128)} %convert_element_type.357, () %tuple.17, (s32[128]{0:T(128)S(1)}, s32[128]{0:T(128)S(1)}, bf16[1,2048,128]{1,2,0:T(8,128)(2,1)S(1)}, bf16[1,2048,128]{1,2,0:T(8,128)(2,1)S(1)}) %tuple.74), branch_computations={%region_0.1_spmd, %region_1.3_spmd} | conditional | flops 5402838528 | bytes 54119660 | solution.py:131
  74.5 16.1 %fusion.71 = bf16[512,256]{0,1:T(8,128)(2,1)S(1)} fusion(bf16[2048,256]{0,1:T(8,128)(2,1)S(1)} %bitcast.183, s32[512]{0:T(512)S(1)} %iota_add_fusion.2), kind=kOutput, calls=%fused_computation.85 | convolution fusion | flops 552861696 | bytes 1312768 | tf_op jit(solution)/shard_map/cond/branch_1_fun/dot_general | solution.py:36
  90.8 18.3 %fusion.72 = bf16[512,256]{0,1:T(8,128)(2,1)} fusion(bf16[2048,256]{0,1:T(8,128)(2,1)} %bitcast.184, s32[512]{0:T(512)S(1)} %iota_add_fusion.1), kind=kOutput, calls=%fused_computation.86 | convolution fusion | flops 552861696 | bytes 1312768 | tf_op jit(solution)/shard_map/cond/branch_1_fun/dot_general | solution.py:36
  109.1 1.8 copy.15
  110.9 17.8 %fusion.73 = bf16[512,256]{0,1:T(8,128)(2,1)} fusion(bf16[2048,256]{0,1:T(8,128)(2,1)S(1)} %bitcast.185, s32[512]{0:T(512)S(1)} %iota_add_fusion), kind=kOutput, calls=%fused_computation.87 | convolution fusion | flops 552861696 | bytes 1312768 | tf_op jit(solution)/shard_map/cond/branch_1_fun/dot_general | solution.py:36
  128.7 1.8 copy.16
  130.5 16.9 %fusion.67 = bf16[512,256]{0,1:T(8,128)(2,1)} fusion(bf16[2048,256]{0,1:T(8,128)(2,1)S(1)} %bitcast.186), kind=kOutput, calls=%fused_computation.83 | convolution fusion | flops 552861696 | bytes 1310720 | tf_op jit(solution)/shard_map/cond/branch_1_fun/dot_general | solution.py:36
  147.4 1.8 copy.13
  149.2 16.0 %fusion.74 = bf16[512,2,128]{2,0,1:T(8,128)(2,1)S(1)} fusion(s32[512]{0:T(512)S(1)} %iota_add_fusion, bf16[2,2048,128]{1,2,0:T(8,128)(2,1)S(1)} %copy-done.2), kind=kOutput, calls=%fused_computation.88 | convolution fusion | flops 552730624 | bytes 1312768 | tf_op jit(solution)/shard_map/cond/branch_1_fun/dot_general | solution.py:35
  165.2 16.1 %fusion.77 = bf16[512,2,128]{2,0,1:T(8,128)(2,1)S(1)} fusion(s32[512]{0:T(512)S(1)} %iota_add_fusion.1, bf16[2,2048,128]{1,2,0:T(8,128)(2,1)S(1)} %copy-done.2), kind=kOutput, calls=%fused_computation.89 | convolution fusion | flops 552730624 | bytes 1312768 | tf_op jit(solution)/shard_map/cond/branch_1_fun/dot_general | solution.py:35
  181.4 16.3 %fusion.80 = bf16[512,2,128]{2,0,1:T(8,128)(2,1)S(1)} fusion(s32[512]{0:T(512)S(1)} %iota_add_fusion.2, bf16[2,2048,128]{1,2,0:T(8,128)(2,1)S(1)} %copy-done.2), kind=kOutput, calls=%fused_computation.90 | convolution fusion | flops 552730624 | bytes 1312768 | tf_op jit(solution)/shard_map/cond/branch_1_fun/dot_general | solution.py:35
  197.7 16.1 %fusion.68 = bf16[512,2,128]{2,0,1:T(8,128)(2,1)S(1)} fusion(bf16[2,2048,128]{1,2,0:T(8,128)(2,1)S(1)} %copy-done.2), kind=kOutput, calls=%fused_computation.84 | convolution fusion | flops 552730624 | bytes 1310720 | tf_op jit(solution)/shard_map/cond/branch_1_fun/dot_general | solution.py:35
  215.9 2.2 fusion.115
  218.8 1.7 fusion.113
  221.1 4.2 %fusion.112 = bf16[128,2048]{1,0:T(8,128)(2,1)S(1)} fusion(s32[128]{0:T(128)S(1)} %get-tuple-element.28), kind=kLoop, calls=%fused_computation.129 | loop fusion | flops 4718592 | bytes 524800 | tf_op jit(solution)/shard_map/cond/branch_1_fun/neg | solution.py:81
  225.4 4.2 %fusion.87 = bf16[128,2048]{1,0:T(8,128)(2,1)S(1)} fusion(s32[128]{0:T(128)S(1)} %get-tuple-element.28), kind=kLoop, calls=%fused_computation.96 | loop fusion | flops 3932160 | bytes 524800 | tf_op jit(solution)/shard_map/cond/branch_1_fun/convert_element_type | solution.py:19
  230.9 153.3 %conditional.3 = (f32[128,128]{1,0:T(8,128)S(1)}) conditional(s32[]{:T(128)} %convert_element_type.358, () %tuple.19, (s32[128]{0:T(128)S(1)}, s32[128]{0:T(128)S(1)}, bf16[1,1,4,1,2048,128]{5,4,3,2,1,0:T(8,128)(2,1)S(1)}, bf16[1,2048,128]{1,2,0:T(8,128)(2,1)}) %tuple.73), branch_computations={%region_3.4_spmd, %region_4.6_spmd} | conditional | flops 5411751424 | bytes 47565864 | solution.py:132
  230.9 2.7 copy.24
  234.7 1.1 pad_maximum_fusion.6
  235.8 16.1 %fusion.238 = bf16[512,256]{0,1:T(8,128)(2,1)S(1)} fusion(bf16[2048,256]{0,1:T(8,128)(2,1)S(1)} %bitcast.175, s32[512]{0:T(512)S(1)} %iota_add_fusion.5), kind=kOutput, calls=%fused_computation.281 | convolution fusion | flops 552861696 | bytes 1312768 | tf_op jit(solution)/shard_map/cond/branch_1_fun/dot_general | solution.py:36
  252.2 16.5 %fusion.239 = bf16[512,256]{0,1:T(8,128)(2,1)S(1)} fusion(bf16[2048,256]{0,1:T(8,128)(2,1)S(1)} %bitcast.176, s32[512]{0:T(512)S(1)} %iota_add_fusion.4), kind=kOutput, calls=%fused_computation.282 | convolution fusion | flops 552861696 | bytes 1312768 | tf_op jit(solution)/shard_map/cond/branch_1_fun/dot_general | solution.py:36
  268.9 16.3 %fusion.240 = bf16[512,256]{0,1:T(8,128)(2,1)S(1)} fusion(bf16[2048,256]{0,1:T(8,128)(2,1)S(1)} %bitcast.177, s32[512]{0:T(512)S(1)} %iota_add_fusion.3), kind=kOutput, calls=%fused_computation.283 | convolution fusion | flops 552861696 | bytes 1312768 | tf_op jit(solution)/shard_map/cond/branch_1_fun/dot_general | solution.py:36
  285.3 16.7 %fusion.234 = bf16[512,256]{0,1:T(8,128)(2,1)S(1)} fusion(bf16[2048,256]{0,1:T(8,128)(2,1)S(1)} %bitcast.178), kind=kOutput, calls=%fused_computation.279 | convolution fusion | flops 552861696 | bytes 1310720 | tf_op jit(solution)/shard_map/cond/branch_1_fun/dot_general | solution.py:36
  302.3 16.8 %fusion.241 = bf16[512,2,128]{2,0,1:T(8,128)(2,1)S(1)} fusion(s32[512]{0:T(512)S(1)} %iota_add_fusion.3, bf16[1,2048,128]{1,2,0:T(8,128)(2,1)} %get-tuple-element.34, bf16[1,2048,128]{1,2,0:T(8,128)(2,1)S(1)} %slice_bitcast_fusion), kind=kOutput, calls=%fused_computation.284 | convolution fusion | flops 554827776 | bytes 1312768 | tf_op jit(solution)/shard_map/cond/branch_1_fun/dot_general | solution.py:35
  319.1 16.9 %fusion.244 = bf16[512,2,128]{2,0,1:T(8,128)(2,1)S(1)} fusion(s32[512]{0:T(512)S(1)} %iota_add_fusion.4, bf16[1,2048,128]{1,2,0:T(8,128)(2,1)} %get-tuple-element.34, bf16[1,2048,128]{1,2,0:T(8,128)(2,1)S(1)} %slice_bitcast_fusion), kind=kOutput, calls=%fused_computation.285 | convolution fusion | flops 554827776 | bytes 1312768 | tf_op jit(solution)/shard_map/cond/branch_1_fun/dot_general | solution.py:35
  336.0 17.2 %fusion.247 = bf16[512,2,128]{2,0,1:T(8,128)(2,1)S(1)} fusion(s32[512]{0:T(512)S(1)} %iota_add_fusion.5, bf16[1,2048,128]{1,2,0:T(8,128)(2,1)} %get-tuple-element.34, bf16[1,2048,128]{1,2,0:T(8,128)(2,1)S(1)} %slice_bitcast_fusion), kind=kOutput, calls=%fused_computation.286 | convolution fusion | flops 554827776 | bytes 1312768 | tf_op jit(solution)/shard_map/cond/branch_1_fun/dot_general | solution.py:35
  353.2 16.9 %fusion.235 = bf16[512,2,128]{2,0,1:T(8,128)(2,1)S(1)} fusion(bf16[1,2048,128]{1,2,0:T(8,128)(2,1)} %get-tuple-element.34, bf16[1,2048,128]{1,2,0:T(8,128)(2,1)S(1)} %slice_bitcast_fusion), kind=kOutput, calls=%fused_computation.280 | convolution fusion | flops 554827776 | bytes 1310720 | tf_op jit(solution)/shard_map/cond/branch_1_fun/dot_general | solution.py:35
  372.2 1.2 fusion.282
  375.2 4.2 %fusion.254 = bf16[128,2048]{1,0:T(8,128)(2,1)S(1)} fusion(s32[128]{0:T(128)S(1)} %get-tuple-element.32), kind=kLoop, calls=%fused_computation.292 | loop fusion | flops 3932160 | bytes 524800 | tf_op jit(solution)/shard_map/cond/branch_1_fun/convert_element_type | solution.py:19
  379.3 4.2 %fusion.279 = bf16[128,2048]{1,0:T(8,128)(2,1)S(1)} fusion(s32[128]{0:T(128)S(1)} %get-tuple-element.32), kind=kLoop, calls=%fused_computation.326 | loop fusion | flops 4718592 | bytes 524800 | tf_op jit(solution)/shard_map/cond/branch_1_fun/neg | solution.py:81
  384.9 1.9 collective-permute-start.10
  386.8 1.9 collective-permute-start.11
  390.3 3.4 collective-permute-done.10
  (119 shorter events, 24.7 us)
Async XLA Ops:
  1.5 34.2 %copy-start.16 = (s32[16,16]{1,0:T(8,128)S(1)}, s32[16,16]{1,0:T(8,128)}, u32[]{:S(2)}) copy-start(s32[16,16]{1,0:T(8,128)} %param.7) | copy-start | bytes 3076
  1.7 72.5 %collective-permute-start = (bf16[1,2048,128]{1,2,0:T(8,128)(2,1)S(1)}, bf16[1,2048,128]{1,2,0:T(8,128)(2,1)S(1)}, u32[]{:S(2)}, u32[]{:S(2)}) collective-permute-start(bf16[1,2048,128]{1,2,0:T(8,128)(2,1)S(1)} %bitcast.179), channel_id=1, source_target_pairs={{1,0},{2,1},{3,2},{4,3},{5,4},{6,5},{7,6},{8,7},{9,8},{10,9},{11,1... | collective-permute-start | bytes 1572872 | tf_op jit(solution)/shard_map/ppermute | solution.py:12
  9.3 22.3 %collective-permute-start.2 = (bf16[1,128,128]{1,2,0:T(8,128)(2,1)S(1)}, bf16[1,128,128]{1,2,0:T(8,128)(2,1)S(1)}, u32[]{:S(2)}, u32[]{:S(2)}) collective-permute-start(bf16[1,128,128]{1,2,0:T(8,128)(2,1)S(1)} %slice.263), channel_id=1, source_target_pairs={{16,0},{32,16},{48,32},{64,48},{80,64},{96,80},{112,96},{128,112},... | collective-permute-start | bytes 98312 | tf_op jit(solution)/shard_map/ppermute | solution.py:12
  11.6 24.1 %collective-permute-start.4 = (bf16[1,128,128]{1,2,0:T(8,128)(2,1)S(1)}, bf16[1,128,128]{1,2,0:T(8,128)(2,1)S(1)}, u32[]{:S(2)}, u32[]{:S(2)}) collective-permute-start(bf16[1,128,128]{1,2,0:T(8,128)(2,1)S(1)} %get-tuple-element.88), channel_id=1, source_target_pairs={{16,0},{32,16},{48,32},{64,48},{80,64},{96,80},{112,96},{128,112},... | collective-permute-start | bytes 98312 | tf_op jit(solution)/shard_map/ppermute | solution.py:12
  14.5 23.9 %collective-permute-start.6 = (bf16[1,128,128]{1,2,0:T(8,128)(2,1)S(1)}, bf16[1,128,128]{1,2,0:T(8,128)(2,1)S(1)}, u32[]{:S(2)}, u32[]{:S(2)}) collective-permute-start(bf16[1,128,128]{1,2,0:T(8,128)(2,1)S(1)} %get-tuple-element.86), channel_id=1, source_target_pairs={{0,16},{16,32},{32,48},{48,64},{64,80},{80,96},{96,112},{112,128},... | collective-permute-start | bytes 98312 | tf_op jit(solution)/shard_map/ppermute | solution.py:12
  17.4 213.4 %collective-permute-start.1 = (bf16[1,2048,128]{1,2,0:T(8,128)(2,1)}, bf16[1,2048,128]{1,2,0:T(8,128)(2,1)}, u32[]{:S(2)}, u32[]{:S(2)}) collective-permute-start(bf16[1,2048,128]{1,2,0:T(8,128)(2,1)} %bitcast.42), channel_id=1, source_target_pairs={{16,0},{32,16},{48,32},{64,48},{80,64},{96,80},{112,96},{128,112},... | collective-permute-start | bytes 1572872 | tf_op jit(solution)/shard_map/ppermute | solution.py:12
  31.6 9.2 %collective-permute-start.3 = (bf16[1,128,128]{1,2,0:T(8,128)(2,1)S(1)}, bf16[1,128,128]{1,2,0:T(8,128)(2,1)S(1)}, u32[]{:S(2)}, u32[]{:S(2)}) collective-permute-start(bf16[1,128,128]{1,2,0:T(8,128)(2,1)S(1)} %collective-permute-done.2), channel_id=1, source_target_pairs={{1,0},{2,1},{3,2},{4,3},{5,4},{6,5},{7,6},{8,7},{9,8},{10,9},{11,1... | collective-permute-start | bytes 98312 | tf_op jit(solution)/shard_map/ppermute | solution.py:12
  35.7 8.8 %collective-permute-start.5 = (bf16[1,128,128]{1,2,0:T(8,128)(2,1)S(1)}, bf16[1,128,128]{1,2,0:T(8,128)(2,1)S(1)}, u32[]{:S(2)}, u32[]{:S(2)}) collective-permute-start(bf16[1,128,128]{1,2,0:T(8,128)(2,1)S(1)} %collective-permute-done.4), channel_id=1, source_target_pairs={{0,1},{1,2},{2,3},{3,4},{4,5},{5,6},{6,7},{7,8},{8,9},{9,10},{10,1... | collective-permute-start | bytes 98312 | tf_op jit(solution)/shard_map/ppermute | solution.py:12
  38.4 9.2 %collective-permute-start.7 = (bf16[1,128,128]{1,2,0:T(8,128)(2,1)S(1)}, bf16[1,128,128]{1,2,0:T(8,128)(2,1)S(1)}, u32[]{:S(2)}, u32[]{:S(2)}) collective-permute-start(bf16[1,128,128]{1,2,0:T(8,128)(2,1)S(1)} %collective-permute-done.6), channel_id=1, source_target_pairs={{0,1},{1,2},{2,3},{3,4},{4,5},{5,6},{6,7},{7,8},{8,9},{9,10},{10,1... | collective-permute-start | bytes 98312 | tf_op jit(solution)/shard_map/ppermute | solution.py:12
  47.6 5.2 %collective-permute-start.8 = (bf16[1,128,128]{1,2,0:T(8,128)(2,1)S(1)}, bf16[1,128,128]{1,2,0:T(8,128)(2,1)S(1)}, u32[]{:S(2)}, u32[]{:S(2)}) collective-permute-start(bf16[1,128,128]{1,2,0:T(8,128)(2,1)S(1)} %get-tuple-element.84), channel_id=1, source_target_pairs={{0,16},{16,32},{32,48},{48,64},{64,80},{80,96},{96,112},{112,128},... | collective-permute-start | bytes 98312 | tf_op jit(solution)/shard_map/ppermute | solution.py:12
  52.9 11.3 %collective-permute-start.9 = (bf16[1,128,128]{1,2,0:T(8,128)(2,1)S(1)}, bf16[1,128,128]{1,2,0:T(8,128)(2,1)S(1)}, u32[]{:S(2)}, u32[]{:S(2)}) collective-permute-start(bf16[1,128,128]{1,2,0:T(8,128)(2,1)S(1)} %collective-permute-done.8), channel_id=1, source_target_pairs={{1,0},{2,1},{3,2},{4,3},{5,4},{6,5},{7,6},{8,7},{9,8},{10,9},{11,1... | collective-permute-start | bytes 98312 | tf_op jit(solution)/shard_map/ppermute | solution.py:12
  74.2 156.7 %copy-start = (bf16[1,1,4,1,2048,128]{5,4,3,2,1,0:T(8,128)(2,1)S(1)}, bf16[1,1,4,1,2048,128]{5,4,3,2,1,0:T(8,128)(2,1)}, u32[]{:S(2)}) copy-start(bf16[1,1,4,1,2048,128]{5,4,3,2,1,0:T(8,128)(2,1)} %param.6) | copy-start | bytes 6291460
  74.5 16.2 %copy-start.1 = (bf16[2,2048,128]{1,2,0:T(8,128)(2,1)}, bf16[2,2048,128]{1,2,0:T(8,128)(2,1)S(1)}, u32[]{:S(2)}) copy-start(bf16[2,2048,128]{1,2,0:T(8,128)(2,1)S(1)} %constant_dynamic-update-slice_fusion) | copy-start | bytes 3145732 | tf_op jit(solution)/shard_map/cond
  90.8 20.1 %copy-start.2 = (bf16[2,2048,128]{1,2,0:T(8,128)(2,1)S(1)}, bf16[2,2048,128]{1,2,0:T(8,128)(2,1)}, u32[]{:S(2)}) copy-start(bf16[2,2048,128]{1,2,0:T(8,128)(2,1)} %copy-done.1) | copy-start | bytes 3145732 | tf_op jit(solution)/shard_map/cond
  197.7 16.7 %copy-start.3 = (bf16[512,2,128]{2,0,1:T(8,128)(2,1)S(1)}, bf16[512,2,128]{2,0,1:T(8,128)(2,1)}, u32[]{:S(2)}) copy-start(bf16[512,2,128]{2,0,1:T(8,128)(2,1)} %copy.15) | copy-start | bytes 786436 | tf_op jit(solution)/shard_map/cond
  197.7 16.7 %copy-start.4 = (bf16[512,2,128]{2,0,1:T(8,128)(2,1)S(1)}, bf16[512,2,128]{2,0,1:T(8,128)(2,1)}, u32[]{:S(2)}) copy-start(bf16[512,2,128]{2,0,1:T(8,128)(2,1)} %copy.16) | copy-start | bytes 786436 | tf_op jit(solution)/shard_map/cond
  197.7 16.7 %copy-start.5 = (bf16[512,2,128]{2,0,1:T(8,128)(2,1)S(1)}, bf16[512,2,128]{2,0,1:T(8,128)(2,1)}, u32[]{:S(2)}) copy-start(bf16[512,2,128]{2,0,1:T(8,128)(2,1)} %copy.13) | copy-start | bytes 786436 | tf_op jit(solution)/shard_map/cond
  214.3 1.0 copy-start.6
  218.1 2.4 copy-start.7
  230.8 157.9 %copy-start.14 = (bf16[128,128]{1,0:T(8,128)(2,1)S(1)}, bf16[128,128]{1,0:T(8,128)(2,1)}, u32[]{:S(2)}) copy-start(bf16[128,128]{1,0:T(8,128)(2,1)} %get-tuple-element.103) | copy-start | bytes 98308
  230.8 157.9 %copy-start.15 = (bf16[128,128]{1,0:T(8,128)(2,1)S(1)}, bf16[128,128]{1,0:T(8,128)(2,1)}, u32[]{:S(2)}) copy-start(bf16[128,128]{1,0:T(8,128)(2,1)} %get-tuple-element.104) | copy-start | bytes 98308
  230.8 158.7 %copy-start.12 = (bf16[128,128]{1,0:T(8,128)(2,1)S(1)}, bf16[128,128]{1,0:T(8,128)(2,1)}, u32[]{:S(2)}) copy-start(bf16[128,128]{1,0:T(8,128)(2,1)} %get-tuple-element.101) | copy-start | bytes 98308
  230.9 158.7 %copy-start.13 = (bf16[128,128]{1,0:T(8,128)(2,1)S(1)}, bf16[128,128]{1,0:T(8,128)(2,1)}, u32[]{:S(2)}) copy-start(bf16[128,128]{1,0:T(8,128)(2,1)} %get-tuple-element.102) | copy-start | bytes 98308
  230.9 164.1 %copy-start.10 = (bf16[128,128]{1,0:T(8,128)(2,1)S(1)}, bf16[128,128]{1,0:T(8,128)(2,1)}, u32[]{:S(2)}) copy-start(bf16[128,128]{1,0:T(8,128)(2,1)} %get-tuple-element.99) | copy-start | bytes 98308
  230.9 164.1 %copy-start.11 = (bf16[128,128]{1,0:T(8,128)(2,1)S(1)}, bf16[128,128]{1,0:T(8,128)(2,1)}, u32[]{:S(2)}) copy-start(bf16[128,128]{1,0:T(8,128)(2,1)} %get-tuple-element.100) | copy-start | bytes 98308
  230.9 164.9 %copy-start.8 = (bf16[128,128]{1,0:T(8,128)(2,1)S(1)}, bf16[128,128]{1,0:T(8,128)(2,1)}, u32[]{:S(2)}) copy-start(bf16[128,128]{1,0:T(8,128)(2,1)} %get-tuple-element.97) | copy-start | bytes 98308
  230.9 164.9 %copy-start.9 = (bf16[128,128]{1,0:T(8,128)(2,1)S(1)}, bf16[128,128]{1,0:T(8,128)(2,1)}, u32[]{:S(2)}) copy-start(bf16[128,128]{1,0:T(8,128)(2,1)} %get-tuple-element.98) | copy-start | bytes 98308
  384.9 8.8 %collective-permute-start.10 = (bf16[128,128]{1,0:T(8,128)(2,1)S(1)}, bf16[128,128]{1,0:T(8,128)(2,1)S(1)}, u32[]{:S(2)}, u32[]{:S(2)}) collective-permute-start(bf16[128,128]{1,0:T(8,128)(2,1)S(1)} %multiply_convert_fusion.13), channel_id=1, source_target_pairs={{0,1},{1,2},{2,3},{3,4},{4,5},{5,6},{6,7},{7,8},{8,9},{9,10},{10,1... | collective-permute-start | bytes 98312 | tf_op jit(solution)/shard_map/ppermute | solution.py:12
  386.8 7.5 %collective-permute-start.11 = (bf16[128,128]{1,0:T(8,128)(2,1)S(1)}, bf16[128,128]{1,0:T(8,128)(2,1)S(1)}, u32[]{:S(2)}, u32[]{:S(2)}) collective-permute-start(bf16[128,128]{1,0:T(8,128)(2,1)S(1)} %multiply_convert_fusion.12), channel_id=1, source_target_pairs={{0,16},{16,32},{32,48},{48,64},{64,80},{80,96},{96,112},{112,128},... | collective-permute-start | bytes 98312 | tf_op jit(solution)/shard_map/ppermute | solution.py:12
where the time goes:
time: 402 us; the launch traced here: 397 us
  matrix products  276 us (69%)
  starting transfers between devices  36.6 us (9%)
  other arithmetic  32.1 us (8%)
  waiting for transfers between devices  22.5 us (6%)
  local copies, waits for them, and re-layouts  16.5 us (4%)
  between operations  10.9 us (3%)
    dot_general x9, matrix products, along_length(): jnp.dot(sine_table, flattened, preferred_element_type=jnp.float32)  135 us
    dot_general x9, matrix products, along_length(): jnp.dot(cosine, flattened, preferred_element_type=jnp.float32)  133 us
    ppermute x12, starting transfers between devices, from_behind(): lax.ppermute(value, axis, [(source, source + steps) for source in range(i...  36.6 us
    ppermute x12, waiting for transfers between devices, from_behind(): lax.ppermute(value, axis, [(source, source + steps) for source in range(i...  22.5 us
    neg x3, other arithmetic, correlate(): weights = jnp.concatenate([cosine, -sine_table], 1)  8.71 us
    convert_element_type x3, other arithmetic, table_rows(): jnp.cos(angle).astype(jnp.bfloat16)  8.58 us
  transfers between devices with their start and end apart: 12, of which 5 were waited for; matrix products, arithmetic and copies ran while one was open for 42% of the time, Pallas kernels for 0%

commit v1 on v0

v1 whole, which is shorter than its diff:
```python
import functools
import math

import jax
import jax.numpy as jnp
import ml_dtypes
import numpy as np
from jax import lax
from jax.experimental import pallas as pl
from jax.experimental.pallas import tpu as pltpu
from jax.sharding import PartitionSpec as P

MESH = pl.DeviceIdType.MESH
CHUNK = 256
BF16 = jnp.bfloat16
F32 = jnp.float32


def trig(rows, columns, length):
    product = (rows[:, None].astype(np.int64) * columns[None, :]) % length
    angle = (product.astype(np.float32) * np.float32(2.0 * math.pi / length)).astype(np.float64)
    return np.cos(angle), np.sin(angle)


def half_rows(length):
    return -(-(length // 2 + 1) // 16) * 16


def forward_table(length):
    rows = np.arange(half_rows(length))
    cosine, sine = trig(rows, np.arange(length), length)
    keep = (rows <= length // 2)[:, None]
    return np.concatenate([cosine * keep, -sine * keep], 0).astype(ml_dtypes.bfloat16)


def inverse_table(shifts, length):
    rows = np.arange(half_rows(length))
    weight = np.where((rows == 0) | (rows == length // 2), 1.0, 2.0) * (rows <= length // 2)
    cosine, sine = trig(shifts % length, rows, length)
    cosine = cosine.astype(ml_dtypes.bfloat16).astype(np.float64)
    sine = sine.astype(ml_dtypes.bfloat16).astype(np.float64)
    return np.concatenate([cosine * weight, -sine * weight], 1).astype(ml_dtypes.bfloat16)


def spin(breadth):
    cosine, sine = trig(np.arange(breadth), np.arange(breadth), breadth)
    forward = np.block([[cosine, -sine], [sine, cosine]])
    back = np.block([[cosine, sine], [-sine, cosine]])
    return np.stack([forward, back]).astype(ml_dtypes.bfloat16)


def kernel(
    rows, cols, length, breadth,
    strips, occ, table, inverse, corner_table, corner_inverse, spins, out,
    tab, inv_tab, ctab, cinv_tab, spin_v, occ_s, own, got, corner_own, corner_got,
    acc, g_re, g_im, g_inv, z_all, map_out, map_in, out_v,
    tab_sem, small_sem, own_sem, corner_sem, send_sem, recv_sem,
    csend_sem, crecv_sem, msend_sem, mrecv_sem, out_sem,
):
    chunks = length // CHUNK
    half = half_rows(length)
    chalf = half_rows(breadth)
    row = lax.axis_index("row")
    col = lax.axis_index("col")
    parity = lax.rem(row, 2)
    up, down = lax.rem(row + rows - 1, rows), lax.rem(row + 1, rows)
    left, right = lax.rem(col + cols - 1, cols), lax.rem(col + 1, cols)

    barrier = pltpu.get_barrier_semaphore()
    neighbours = [
        (up, left), (up, col), (up, right), (row, left),
        (row, right), (down, left), (down, col), (down, right),
    ]
    for neighbour in neighbours:
        pl.semaphore_signal(barrier, inc=1, device_id=neighbour, device_id_type=MESH)

    small = [
        pltpu.make_async_copy(corner_table, ctab, small_sem.at[0]),
        pltpu.make_async_copy(spins, spin_v, small_sem.at[1]),
        pltpu.make_async_copy(corner_inverse, cinv_tab, small_sem.at[2]),
        pltpu.make_async_copy(inverse, inv_tab, small_sem.at[3]),
        pltpu.make_async_copy(occ, occ_s, small_sem.at[4]),
    ]
    low = pl.ds(length - breadth, breadth)
    top = pl.ds(0, breadth)
    corner_places = [(0, low), (1, low), (1, top), (0, top)]
    corner_loads = [
        pltpu.make_async_copy(strips.at[s, place], corner_own.at[k], corner_sem.at[k])
        for k, (s, place) in enumerate(corner_places)
    ]
    own_loads = [
        pltpu.make_async_copy(strips.at[2], own.at[0], own_sem.at[0]),
        pltpu.make_async_copy(strips.at[parity], own.at[1], own_sem.at[1]),
    ]

    def table_load(c):
        return pltpu.make_async_copy(table.at[c], tab.at[c], tab_sem.at[c])

    for copy in small + corner_loads + own_loads:
        copy.start()
    for c in range(chunks):
        table_load(c).start()

    pl.semaphore_wait(barrier, len(neighbours))

    side = jnp.where(parity == 0, left, right)
    other_side = jnp.where(parity == 0, right, left)

    def strip_copy(idx, c):
        piece = pl.ds(c * CHUNK if isinstance(c, int) else pl.multiple_of(c * CHUNK, CHUNK), CHUNK)
        source = jnp.where(idx == 0, 3, 1 - parity)
        target = (jnp.where(idx == 0, up, row), jnp.where(idx == 0, col, side))
        return pltpu.make_async_remote_copy(
            src_ref=strips.at[source, piece],
            dst_ref=got.at[idx, piece],
            send_sem=send_sem.at[idx, c],
            recv_sem=recv_sem.at[idx, c],
            device_id=target,
            device_id_type=MESH,
        )

    def corner_copy(k):
        target = [(down, right), (down, left), (up, left), (up, right)][k]
        s, place = corner_places[k]
        return pltpu.make_async_remote_copy(
            src_ref=strips.at[s, place],
            dst_ref=corner_got.at[(k + 2) % 4],
            send_sem=csend_sem.at[k],
            recv_sem=crecv_sem.at[(k + 2) % 4],
            device_id=target,
            device_id_type=MESH,
        )

    for k in range(4):
        corner_copy(k).start()
    for idx in (1, 0):
        def start(c, carry, idx=idx):
            strip_copy(idx, c).start()
            return carry
        lax.fori_loop(0, chunks, start, 0)

    for copy in small:
        copy.wait()

    def alive(r1, c1, dr, dc):
        r2, c2 = r1 + dr, c1 + dc
        inside = (r2 >= 0) & (r2 < rows) & (c2 >= 0) & (c2 < cols)
        second = occ_s[lax.rem(r2 + rows, rows), lax.rem(c2 + cols, cols)]
        return (occ_s[r1, c1] * second * jnp.where(inside, 1, 0)).astype(F32)


    def correlate(base, size, block, n, sign, inv_ref, shift_count):
        steps = size // block

        def cross(b, total):
            at = pl.multiple_of(b * block, block)
            c_part = acc[pl.ds(base + at, block), :]
            s_part = acc[pl.ds(base + size + at, block), :]
            halves = jnp.concatenate(
                [
                    jnp.concatenate([c_part[:, :breadth], s_part[:, :breadth]], 1),
                    jnp.concatenate([c_part[:, breadth:], s_part[:, breadth:]], 1),
                ],
                0,
            ).astype(BF16)
            y = jnp.dot(halves, spin_v[0], preferred_element_type=F32).astype(BF16).astype(F32)
            a_re, a_im = y[:block, :breadth], y[:block, breadth:]
            b_re, b_im = y[block:, :breadth], y[block:, breadth:]
            re = a_re * b_re + a_im * b_im
            im = a_im * b_re - a_re * b_im
            square = re * re + im * im
            inverse_m = lax.rsqrt(jnp.maximum(square, 1e-36))
            g_re[pl.ds(at, block), :] = re
            g_im[pl.ds(at, block), :] = im
            g_inv[pl.ds(at, block), :] = inverse_m
            k = lax.broadcasted_iota(jnp.int32, (block, breadth), 0) + at
            weight = jnp.where((k == 0) | (k == n // 2), 1.0, 2.0)
            m = square * inverse_m * weight
            return total + jnp.sum(m.reshape(block // 8, 8, breadth), 0)

        total = lax.fori_loop(0, steps, cross, jnp.zeros((8, breadth), F32))
        floor = 0.5 * (jnp.sum(total, keepdims=True) / (n * breadth)) + 1e-6
        most = 1.0 / floor

        def back(b, carry):
            at = pl.multiple_of(b * block, block)
            scale = jnp.minimum(g_inv[pl.ds(at, block), :], most)
            r = jnp.concatenate(
                [g_re[pl.ds(at, block), :] * scale, g_im[pl.ds(at, block), :] * (scale * sign)], 1
            ).astype(BF16)
            z = jnp.dot(r, spin_v[1], preferred_element_type=F32).astype(BF16)
            z_all[pl.ds(at, block), :] = z[:, :breadth]
            z_all[pl.ds(size + at, block), :] = z[:, breadth:]
            return carry

        lax.fori_loop(0, steps, back, 0)
        return jnp.dot(inv_ref[...], z_all[pl.ds(0, 2 * size), :], preferred_element_type=F32)

    def length_step(idx, c, first):
        piece = pl.ds(c * CHUNK if isinstance(c, int) else pl.multiple_of(c * CHUNK, CHUNK), CHUNK)
        strip_copy(idx, c).wait_recv()
        x = jnp.concatenate([own[idx, piece, :], got[idx, piece, :]], 1)
        rows_at = 2 * half // 5

        def part(b, carry):
            at = pl.ds(pl.multiple_of(b * rows_at, 16), rows_at)
            product = jnp.dot(tab[c, at, :], x, preferred_element_type=F32)
            if first:
                acc[at, :] = product
            else:
                acc[at, :] += product
            return carry

        lax.fori_loop(0, 5, part, 0)

    def corners():
        scale = 1.0 / math.sqrt(breadth * breadth)
        steps = [(1, 1), (1, -1), (-1, -1), (-1, 1)]
        for k in range(4):
            corner_loads[k].wait()
            corner_copy((k + 2) % 4).wait_recv()
            x = jnp.concatenate([corner_own[k], corner_got[k]], 1)
            acc[pl.ds(0, 2 * chalf), :] = jnp.dot(ctab[...], x, preferred_element_type=F32)
            result = correlate(0, chalf, chalf, breadth, 1.0 if k < 2 else -1.0, cinv_tab, breadth)
            slot = (2, 3, 6, 7)[k]
            out_v[slot] = result * (alive(row, col, *steps[k]) * scale)
            out_copy(slot).start()

    def out_copy(slot):
        return pltpu.make_async_copy(out_v.at[slot], out.at[slot], out_sem.at[slot])

    def map_copy(idx):
        target = (jnp.where(idx == 0, down, row), jnp.where(idx == 0, col, other_side))
        return pltpu.make_async_remote_copy(
            src_ref=map_out.at[idx],
            dst_ref=map_in.at[idx],
            send_sem=msend_sem.at[idx],
            recv_sem=mrecv_sem.at[idx],
            device_id=target,
            device_id_type=MESH,
        )

    for copy in own_loads:
        copy.wait()

    def phase(p, carry):
        idx = lax.rem(p + parity, 2)

        @pl.when(p == 0)
        def _():
            table_load(0).wait()

        length_step(idx, 0, True)

        def more(c, inner):
            @pl.when(p == 0)
            def _():
                table_load(c).wait()

            length_step(idx, c, False)
            return inner

        lax.fori_loop(1, chunks, more, 0)
        sign = jnp.where(idx == 0, 1, 1 - 2 * parity).astype(F32)
        result = correlate(0, half, half // 5, length, sign, inv_tab, breadth)
        live = alive(
            row, col, jnp.where(idx == 0, 1, 0), jnp.where(idx == 0, 0, 1 - 2 * parity)
        )
        result = result * (live * (1.0 / math.sqrt(length * breadth)))
        map_out[idx] = result.astype(BF16)
        map_copy(idx).start()
        slot = jnp.where(idx == 0, 1, 4 * parity)
        out_v[slot] = result
        out_copy(slot).start()

        @pl.when(p == 0)
        def _():
            corners()

        return carry

    lax.fori_loop(0, 2, phase, 0)

    for idx in (1, 0):
        map_copy(idx).wait_recv()
        slot = 4 * (1 - parity) if idx == 1 else 5
        out_v[slot] = map_in[idx].astype(F32)
        out_copy(slot).start()

    for idx in (1, 0):
        map_copy(idx).wait_send()

        def sent(c, carry, idx=idx):
            strip_copy(idx, c).wait_send()
            return carry

        lax.fori_loop(0, chunks, sent, 0)
    for k in range(4):
        corner_copy(k).wait_send()
    for slot in range(8):
        out_copy(slot).wait()


def per_device(rows, cols, strips, occupancy):
    length, breadth = strips.shape[4:]
    chunks = length // CHUNK
    half, chalf = half_rows(length), half_rows(breadth)
    forward = forward_table(length)
    table = jnp.asarray(
        np.ascontiguousarray(forward.reshape(2 * half, chunks, CHUNK).transpose(1, 0, 2))
    )
    inverse = jnp.asarray(inverse_table(np.arange(breadth) - breadth // 2, length))
    corner_table = jnp.asarray(forward_table(breadth))
    corner_inverse = jnp.asarray(inverse_table(np.arange(breadth), breadth))
    spins = jnp.asarray(spin(breadth))
    hbm = pl.BlockSpec(memory_space=pl.ANY)
    dma = pltpu.SemaphoreType.DMA
    result = pl.pallas_call(
        functools.partial(kernel, rows, cols, length, breadth),
        out_shape=jax.ShapeDtypeStruct((8, breadth, breadth), F32),
        in_specs=[hbm] * 7,
        out_specs=hbm,
        scratch_shapes=[
            pltpu.VMEM((chunks, 2 * half, CHUNK), BF16),
            pltpu.VMEM((breadth, 2 * half), BF16),
            pltpu.VMEM((2 * chalf, breadth), BF16),
            pltpu.VMEM((breadth, 2 * chalf), BF16),
            pltpu.VMEM((2, 2 * breadth, 2 * breadth), BF16),
            pltpu.SMEM((rows, cols), jnp.int32),
            pltpu.VMEM((2, length, breadth), BF16),
            pltpu.VMEM((2, length, breadth), BF16),
            pltpu.VMEM((4, breadth, breadth), BF16),
            pltpu.VMEM((4, breadth, breadth), BF16),
            pltpu.VMEM((2 * half, 2 * breadth), F32),
            pltpu.VMEM((half, breadth), F32),
            pltpu.VMEM((half, breadth), F32),
            pltpu.VMEM((half, breadth), F32),
            pltpu.VMEM((2 * half, breadth), BF16),
            pltpu.VMEM((2, breadth, breadth), BF16),
            pltpu.VMEM((2, breadth, breadth), BF16),
            pltpu.VMEM((8, breadth, breadth), F32),
            dma((chunks,)),
            dma((5,)),
            dma((2,)),
            dma((4,)),
            dma((2, chunks)),
            dma((2, chunks)),
            dma((4,)),
            dma((4,)),
            dma((2,)),
            dma((2,)),
            dma((8,)),
        ],
        compiler_params=pltpu.CompilerParams(
            collective_id=0, has_side_effects=True, vmem_limit_bytes=40 * 1024 * 1024
        ),
    )(
        strips.reshape(4, length, breadth), occupancy, table, inverse, corner_table,
        corner_inverse, spins,
    )
    return result[None, None]


def solution(mesh):
    rows, cols = mesh.shape["row"], mesh.shape["col"]
    return jax.shard_map(
        functools.partial(per_device, rows, cols),
        mesh=mesh,
        in_specs=(P("row", "col", None, None, None, None), P()),
        out_specs=P("row", "col", None, None, None),
        check_vma=False,
    )
```

time: 402 us -> 61.2 us (0.15)
  the two profiles are of different devices: /device:TPU:54 before, /device:TPU:1 now
where the time goes in v1:
time: 61.2 us; the launch traced here: 60.3 us
  Pallas kernels  50.2 us (82%)
  local copies, waits for them, and re-layouts  10.1 us (17%)
    pallas_call x1, Pallas kernels, per_device(): pl.pallas_call(functools.partial(kernel, rows, cols, length, breadth), ou...  50.2 us
    unnamed x15, local copies, waits for them, and re-layouts  10.1 us

profile of v1, /device:TPU:1, one launch (start us, length us, event | category | flops | bytes accessed | tf_op | source)
XLA Modules:
  0.0 60.3 jit_solution(4959406260640976771)
XLA Ops:
  0.0 0.0 copy-start
  0.0 3.4 %copy-done = bf16[8,2080,256]{2,1,0:T(8,128)(2,1)S(1)} copy-done((bf16[8,2080,256]{2,1,0:T(8,128)(2,1)S(1)}, bf16[8,2080,256]{2,1,0:T(8,128)(2,1)}, u32[]{:S(2)}) %copy-start) | copy-done | bytes 8519704
  3.4 0.0 copy-start.1
  3.4 1.6 %copy-done.1 = bf16[1,1,4,1,2048,128]{5,4,3,2,1,0:T(8,128)(2,1)S(1)} copy-done((bf16[1,1,4,1,2048,128]{5,4,3,2,1,0:T(8,128)(2,1)S(1)}, bf16[1,1,4,1,2048,128]{5,4,3,2,1,0:T(8,128)(2,1)}, u32[]{:S(2)}) %copy-start.1) | copy-done | bytes 2097176
  5.0 0.0 copy-start.2
  5.0 1.1 %copy-done.2 = bf16[128,2080]{1,0:T(8,128)(2,1)S(1)} copy-done((bf16[128,2080]{1,0:T(8,128)(2,1)S(1)}, bf16[128,2080]{1,0:T(8,128)(2,1)}, u32[]{:S(2)}) %copy-start.2) | copy-done | bytes 532504
  6.1 0.0 copy-start.3
  6.1 0.9 %copy-done.3 = bf16[2,256,256]{2,1,0:T(8,128)(2,1)S(1)} copy-done((bf16[2,256,256]{2,1,0:T(8,128)(2,1)S(1)}, bf16[2,256,256]{2,1,0:T(8,128)(2,1)}, u32[]{:S(2)}) %copy-start.3) | copy-done | bytes 262168
  7.0 0.0 copy-start.4
  7.0 0.8 %copy-done.4 = bf16[128,160]{1,0:T(8,128)(2,1)S(1)} copy-done((bf16[128,160]{1,0:T(8,128)(2,1)S(1)}, bf16[128,160]{1,0:T(8,128)(2,1)}, u32[]{:S(2)}) %copy-start.4) | copy-done | bytes 40984
  7.9 0.0 copy-start.5
  7.9 0.8 %copy-done.5 = bf16[160,128]{1,0:T(8,128)(2,1)S(1)} copy-done((bf16[160,128]{1,0:T(8,128)(2,1)S(1)}, bf16[160,128]{1,0:T(8,128)(2,1)}, u32[]{:S(2)}) %copy-start.5) | copy-done | bytes 40984
  8.6 0.0 copy-start.6
  8.6 0.7 %copy-done.6 = s32[16,16]{1,0:T(8,128)S(1)} copy-done((s32[16,16]{1,0:T(8,128)S(1)}, s32[16,16]{1,0:T(8,128)}, u32[]{:S(2)}) %copy-start.6) | copy-done | bytes 1048
  9.3 50.2 %shard_map.73 = f32[8,128,128]{2,1,0:T(8,128)S(1)} custom-call(bf16[4,2048,128]{2,1,0:T(8,128)(2,1)S(1)} %bitcast.3, s32[16,16]{1,0:T(8,128)S(1)} %copy-done.6, bf16[8,2080,256]{2,1,0:T(8,128)(2,1)S(1)} %copy-done, bf16[128,2080]{1,0:T(8,128)(2,1)S(1)} %copy-done.2, bf16[160,128]{1,0:T(8,128)(2,1)S(1)} %copy-done.5, bf16[128,160]{1,0:T(8,128)(2,1)S(1)} %copy-done.4, ...), custom_call_target="tpu_custom_call" | custom-call | tf_op jit(solution)/shard_map/pallas_call | solution.py:318
  59.5 0.8 %copy.9 = f32[1,1,8,128,128]{4,3,2,1,0:T(8,128)} copy(f32[1,1,8,128,128]{4,3,2,1,0:T(8,128)S(1)} %bitcast.2) | data formatting | bytes 1048576
Async XLA Ops:
  0.0 3.4 %copy-start = (bf16[8,2080,256]{2,1,0:T(8,128)(2,1)S(1)}, bf16[8,2080,256]{2,1,0:T(8,128)(2,1)}, u32[]{:S(2)}) copy-start(bf16[8,2080,256]{2,1,0:T(8,128)(2,1)} %constant.10.clone.table) | copy-start | bytes 25559044
  3.4 1.6 %copy-start.1 = (bf16[1,1,4,1,2048,128]{5,4,3,2,1,0:T(8,128)(2,1)S(1)}, bf16[1,1,4,1,2048,128]{5,4,3,2,1,0:T(8,128)(2,1)}, u32[]{:S(2)}) copy-start(bf16[1,1,4,1,2048,128]{5,4,3,2,1,0:T(8,128)(2,1)} %param.7) | copy-start | bytes 6291460
  5.0 1.1 %copy-start.2 = (bf16[128,2080]{1,0:T(8,128)(2,1)S(1)}, bf16[128,2080]{1,0:T(8,128)(2,1)}, u32[]{:S(2)}) copy-start(bf16[128,2080]{1,0:T(8,128)(2,1)} %constant.11.clone.inverse) | copy-start | bytes 1597444
  6.1 0.9 %copy-start.3 = (bf16[2,256,256]{2,1,0:T(8,128)(2,1)S(1)}, bf16[2,256,256]{2,1,0:T(8,128)(2,1)}, u32[]{:S(2)}) copy-start(bf16[2,256,256]{2,1,0:T(8,128)(2,1)} %constant.14.clone.spins) | copy-start | bytes 786436
  7.0 0.8 %copy-start.4 = (bf16[128,160]{1,0:T(8,128)(2,1)S(1)}, bf16[128,160]{1,0:T(8,128)(2,1)}, u32[]{:S(2)}) copy-start(bf16[128,160]{1,0:T(8,128)(2,1)} %constant.13.clone.corner_inverse) | copy-start | bytes 122884
  7.9 0.8 %copy-start.5 = (bf16[160,128]{1,0:T(8,128)(2,1)S(1)}, bf16[160,128]{1,0:T(8,128)(2,1)}, u32[]{:S(2)}) copy-start(bf16[160,128]{1,0:T(8,128)(2,1)} %constant.12.clone.corner_table) | copy-start | bytes 122884
  8.6 0.7 %copy-start.6 = (s32[16,16]{1,0:T(8,128)S(1)}, s32[16,16]{1,0:T(8,128)}, u32[]{:S(2)}) copy-start(s32[16,16]{1,0:T(8,128)} %occ.1) | copy-start | bytes 3076

commit v2 on v1

--- a/solution.py
+++ b/solution.py
@@ -11,7 +11,9 @@
 from jax.sharding import PartitionSpec as P
 
 MESH = pl.DeviceIdType.MESH
-CHUNK = 256
+CHUNK = 512
+WIDE = 256
+BLOCKS = 5
 BF16 = jnp.bfloat16
 F32 = jnp.float32
 
@@ -49,9 +51,36 @@
     return np.stack([forward, back]).astype(ml_dtypes.bfloat16)
 
 
+def table_places(length, breadth):
+    sizes = [
+        (length // WIDE) * 2 * half_rows(length),
+        4 * breadth,
+        -(-2 * half_rows(length) // WIDE) * breadth,
+        2 * half_rows(breadth),
+        breadth,
+    ]
+    return [(sum(sizes[:k]), size) for k, size in enumerate(sizes)]
+
+
+def packed_tables(length, breadth):
+    def blocks(array):
+        rows, columns = array.shape
+        array = np.pad(array, ((0, 0), (0, -columns % WIDE)))
+        return array.reshape(rows, -1, WIDE).transpose(1, 0, 2).reshape(-1, WIDE)
+
+    parts = [
+        forward_table(length),
+        spin(breadth).reshape(4 * breadth, 2 * breadth),
+        inverse_table(np.arange(breadth) - breadth // 2, length),
+        forward_table(breadth),
+        inverse_table(np.arange(breadth), breadth),
+    ]
+    return np.concatenate([blocks(part) for part in parts], 0)
+
+
 def kernel(
     rows, cols, length, breadth,
-    strips, occ, table, inverse, corner_table, corner_inverse, spins, out,
+    strips, occ, tables, out,
     tab, inv_tab, ctab, cinv_tab, spin_v, occ_s, own, got, corner_own, corner_got,
     acc, g_re, g_im, g_inv, z_all, map_out, map_in, out_v,
     tab_sem, small_sem, own_sem, corner_sem, send_sem, recv_sem,
@@ -74,13 +103,12 @@
     for neighbour in neighbours:
         pl.semaphore_signal(barrier, inc=1, device_id=neighbour, device_id_type=MESH)
 
+    places = table_places(length, breadth)
     small = [
-        pltpu.make_async_copy(corner_table, ctab, small_sem.at[0]),
-        pltpu.make_async_copy(spins, spin_v, small_sem.at[1]),
-        pltpu.make_async_copy(corner_inverse, cinv_tab, small_sem.at[2]),
-        pltpu.make_async_copy(inverse, inv_tab, small_sem.at[3]),
-        pltpu.make_async_copy(occ, occ_s, small_sem.at[4]),
-    ]
+        pltpu.make_async_copy(tables.at[pl.ds(*places[k + 1])], dest, small_sem.at[k])
+        for k, dest in enumerate((spin_v, inv_tab, ctab, cinv_tab))
+    ]
+    small.append(pltpu.make_async_copy(occ, occ_s, small_sem.at[4]))
     low = pl.ds(length - breadth, breadth)
     top = pl.ds(0, breadth)
     corner_places = [(0, low), (1, low), (1, top), (0, top)]
@@ -94,11 +122,14 @@
     ]
 
     def table_load(c):
-        return pltpu.make_async_copy(table.at[c], tab.at[c], tab_sem.at[c])
+        at = pl.multiple_of(c * (2 * half), 16)
+        return pltpu.make_async_copy(
+            tables.at[pl.ds(at, 2 * half)], tab.at[c], tab_sem.at[c]
+        )
 
     for copy in small + corner_loads + own_loads:
         copy.start()
-    for c in range(chunks):
+    for c in range(length // WIDE):
         table_load(c).start()
 
     pl.semaphore_wait(barrier, len(neighbours))
@@ -133,11 +164,18 @@
 
     for k in range(4):
         corner_copy(k).start()
-    for idx in (1, 0):
-        def start(c, carry, idx=idx):
+    def send(idx):
+        def start(c, carry):
             strip_copy(idx, c).start()
             return carry
+
         lax.fori_loop(0, chunks, start, 0)
+
+    send(1)
+
+    @pl.when(parity == 1)
+    def _():
+        send(0)
 
     for copy in small:
         copy.wait()
@@ -149,69 +187,74 @@
         return (occ_s[r1, c1] * second * jnp.where(inside, 1, 0)).astype(F32)
 
 
-    def correlate(base, size, block, n, sign, inv_ref, shift_count):
-        steps = size // block
-
-        def cross(b, total):
-            at = pl.multiple_of(b * block, block)
-            c_part = acc[pl.ds(base + at, block), :]
-            s_part = acc[pl.ds(base + size + at, block), :]
-            halves = jnp.concatenate(
-                [
-                    jnp.concatenate([c_part[:, :breadth], s_part[:, :breadth]], 1),
-                    jnp.concatenate([c_part[:, breadth:], s_part[:, breadth:]], 1),
-                ],
-                0,
-            ).astype(BF16)
-            y = jnp.dot(halves, spin_v[0], preferred_element_type=F32).astype(BF16).astype(F32)
-            a_re, a_im = y[:block, :breadth], y[:block, breadth:]
-            b_re, b_im = y[block:, :breadth], y[block:, breadth:]
-            re = a_re * b_re + a_im * b_im
-            im = a_im * b_re - a_re * b_im
-            square = re * re + im * im
-            inverse_m = lax.rsqrt(jnp.maximum(square, 1e-36))
-            g_re[pl.ds(at, block), :] = re
-            g_im[pl.ds(at, block), :] = im
-            g_inv[pl.ds(at, block), :] = inverse_m
-            k = lax.broadcasted_iota(jnp.int32, (block, breadth), 0) + at
-            weight = jnp.where((k == 0) | (k == n // 2), 1.0, 2.0)
-            m = square * inverse_m * weight
-            return total + jnp.sum(m.reshape(block // 8, 8, breadth), 0)
-
-        total = lax.fori_loop(0, steps, cross, jnp.zeros((8, breadth), F32))
-        floor = 0.5 * (jnp.sum(total, keepdims=True) / (n * breadth)) + 1e-6
-        most = 1.0 / floor
-
-        def back(b, carry):
-            at = pl.multiple_of(b * block, block)
-            scale = jnp.minimum(g_inv[pl.ds(at, block), :], most)
-            r = jnp.concatenate(
-                [g_re[pl.ds(at, block), :] * scale, g_im[pl.ds(at, block), :] * (scale * sign)], 1
-            ).astype(BF16)
-            z = jnp.dot(r, spin_v[1], preferred_element_type=F32).astype(BF16)
-            z_all[pl.ds(at, block), :] = z[:, :breadth]
-            z_all[pl.ds(size + at, block), :] = z[:, breadth:]
-            return carry
-
-        lax.fori_loop(0, steps, back, 0)
-        return jnp.dot(inv_ref[...], z_all[pl.ds(0, 2 * size), :], preferred_element_type=F32)
+    def cross(c_part, s_part, n, first_row):
+        size = c_part.shape[0]
+        halves = jnp.concatenate(
+            [
+                jnp.concatenate([c_part[:, :breadth], s_part[:, :breadth]], 1),
+                jnp.concatenate([c_part[:, breadth:], s_part[:, breadth:]], 1),
+            ],
+            0,
+        ).astype(BF16)
+        y = jnp.dot(halves, spin_v[: 2 * breadth, :], preferred_element_type=F32).astype(BF16).astype(F32)
+        a_re, a_im = y[:size, :breadth], y[:size, breadth:]
+        b_re, b_im = y[size:, :breadth], y[size:, breadth:]
+        re = a_re * b_re + a_im * b_im
+        im = a_im * b_re - a_re * b_im
+        square = re * re + im * im
+        inverse_m = lax.rsqrt(jnp.maximum(square, 1e-36))
+        m = square * inverse_m
+        first = lax.broadcasted_iota(jnp.int32, (8, breadth), 0)
+        total = jnp.zeros((8, breadth), F32)
+        for at in range(0, size, 8):
+            part = m[at : at + 8]
+            if first_row + at == 0 or first_row + at == n // 2:
+                part = part * jnp.where(first == 0, 0.5, 1.0)
+            total = total + part
+        return re, im, inverse_m, total
+
+    def limit_of(total, n):
+        floor = 0.5 * (jnp.sum(total, keepdims=True) * (2.0 / (n * breadth))) + 1e-6
+        return 1.0 / floor
+
+    def back(re, im, inverse_m, most, sign):
+        scale = jnp.minimum(inverse_m, most)
+        r = jnp.concatenate([re * scale, im * (scale * sign)], 1).astype(BF16)
+        return jnp.dot(r, spin_v[2 * breadth :, :], preferred_element_type=F32).astype(BF16)
+
+    def edge_map(sign):
+        block = half // BLOCKS
+        total = jnp.zeros((8, breadth), F32)
+        for at in range(0, half, block):
+            re, im, inverse_m, part = cross(
+                acc[pl.ds(at, block), :], acc[pl.ds(half + at, block), :], length, at
+            )
+            here = pl.ds(at, block)
+            g_re[here, :], g_im[here, :], g_inv[here, :] = re, im, inverse_m
+            total = total + part
+        most = limit_of(total, length)
+        inv = jnp.concatenate(
+            [inv_tab[pl.ds(at, breadth), :] for at in range(0, inv_tab.shape[0], breadth)], 1
+        )[:, : 2 * half]
+        for at in range(0, half, block):
+            here = pl.ds(at, block)
+            z = back(g_re[here, :], g_im[here, :], g_inv[here, :], most, sign)
+            z_all[here, :] = z[:, :breadth]
+            z_all[pl.ds(half + at, block), :] = z[:, breadth:]
+        return jnp.dot(inv, z_all[...], preferred_element_type=F32)
 
     def length_step(idx, c, first):
         piece = pl.ds(c * CHUNK if isinstance(c, int) else pl.multiple_of(c * CHUNK, CHUNK), CHUNK)
         strip_copy(idx, c).wait_recv()
         x = jnp.concatenate([own[idx, piece, :], got[idx, piece, :]], 1)
-        rows_at = 2 * half // 5
-
-        def part(b, carry):
-            at = pl.ds(pl.multiple_of(b * rows_at, 16), rows_at)
-            product = jnp.dot(tab[c, at, :], x, preferred_element_type=F32)
-            if first:
-                acc[at, :] = product
-            else:
-                acc[at, :] += product
-            return carry
-
-        lax.fori_loop(0, 5, part, 0)
+        step = jnp.concatenate(
+            [tab[c * (CHUNK // WIDE) + k] for k in range(CHUNK // WIDE)], 1
+        )
+        product = jnp.dot(step, x, preferred_element_type=F32)
+        if first:
+            acc[...] = product
+        else:
+            acc[...] += product
 
     def corners():
         scale = 1.0 / math.sqrt(breadth * breadth)
@@ -219,11 +262,22 @@
         for k in range(4):
             corner_loads[k].wait()
             corner_copy((k + 2) % 4).wait_recv()
-            x = jnp.concatenate([corner_own[k], corner_got[k]], 1)
-            acc[pl.ds(0, 2 * chalf), :] = jnp.dot(ctab[...], x, preferred_element_type=F32)
-            result = correlate(0, chalf, chalf, breadth, 1.0 if k < 2 else -1.0, cinv_tab, breadth)
+        x = jnp.concatenate(
+            [part for k in range(4) for part in (corner_own[k], corner_got[k])], 1
+        )
+        product = jnp.dot(ctab[:, :breadth], x, preferred_element_type=F32)
+        parts = []
+        for k in range(4):
+            wide = product[:, 2 * breadth * k : 2 * breadth * (k + 1)]
+            re, im, inverse_m, total = cross(wide[:chalf], wide[chalf:], breadth, 0)
+            z = back(re, im, inverse_m, limit_of(total, breadth), 1.0 if k < 2 else -1.0)
+            parts.append(jnp.concatenate([z[:, :breadth], z[:, breadth:]], 0))
+        maps = jnp.dot(cinv_tab[:, : 2 * chalf], jnp.concatenate(parts, 1), preferred_element_type=F32)
+        for k in range(4):
             slot = (2, 3, 6, 7)[k]
-            out_v[slot] = result * (alive(row, col, *steps[k]) * scale)
+            out_v[slot] = maps[:, breadth * k : breadth * (k + 1)] * (
+                alive(row, col, *steps[k]) * scale
+            )
             out_copy(slot).start()
 
     def out_copy(slot):
@@ -243,26 +297,34 @@
     for copy in own_loads:
         copy.wait()
 
+    corners()
+
+    @pl.when(parity == 0)
+    def _():
+        send(0)
+
     def phase(p, carry):
         idx = lax.rem(p + parity, 2)
 
         @pl.when(p == 0)
         def _():
-            table_load(0).wait()
+            for k in range(CHUNK // WIDE):
+                table_load(k).wait()
 
         length_step(idx, 0, True)
 
         def more(c, inner):
             @pl.when(p == 0)
             def _():
-                table_load(c).wait()
+                for k in range(CHUNK // WIDE):
+                    table_load(c * (CHUNK // WIDE) + k).wait()
 
             length_step(idx, c, False)
             return inner
 
         lax.fori_loop(1, chunks, more, 0)
         sign = jnp.where(idx == 0, 1, 1 - 2 * parity).astype(F32)
-        result = correlate(0, half, half // 5, length, sign, inv_tab, breadth)
+        result = edge_map(sign)
         live = alive(
             row, col, jnp.where(idx == 0, 1, 0), jnp.where(idx == 0, 0, 1 - 2 * parity)
         )
@@ -272,11 +334,6 @@
         slot = jnp.where(idx == 0, 1, 4 * parity)
         out_v[slot] = result
         out_copy(slot).start()
-
-        @pl.when(p == 0)
-        def _():
-            corners()
-
         return carry
 
     lax.fori_loop(0, 2, phase, 0)
@@ -305,27 +362,21 @@
     length, breadth = strips.shape[4:]
     chunks = length // CHUNK
     half, chalf = half_rows(length), half_rows(breadth)
-    forward = forward_table(length)
-    table = jnp.asarray(
-        np.ascontiguousarray(forward.reshape(2 * half, chunks, CHUNK).transpose(1, 0, 2))
-    )
-    inverse = jnp.asarray(inverse_table(np.arange(breadth) - breadth // 2, length))
-    corner_table = jnp.asarray(forward_table(breadth))
-    corner_inverse = jnp.asarray(inverse_table(np.arange(breadth), breadth))
-    spins = jnp.asarray(spin(breadth))
-    hbm = pl.BlockSpec(memory_space=pl.ANY)
+    tables = jnp.asarray(packed_tables(length, breadth))
+    places = table_places(length, breadth)
+    hbm = pl.BlockSpec(memory_space=pltpu.HBM)
     dma = pltpu.SemaphoreType.DMA
     result = pl.pallas_call(
         functools.partial(kernel, rows, cols, length, breadth),
         out_shape=jax.ShapeDtypeStruct((8, breadth, breadth), F32),
-        in_specs=[hbm] * 7,
+        in_specs=[hbm] * 3,
         out_specs=hbm,
         scratch_shapes=[
-            pltpu.VMEM((chunks, 2 * half, CHUNK), BF16),
-            pltpu.VMEM((breadth, 2 * half), BF16),
-            pltpu.VMEM((2 * chalf, breadth), BF16),
-            pltpu.VMEM((breadth, 2 * chalf), BF16),
-            pltpu.VMEM((2, 2 * breadth, 2 * breadth), BF16),
+            pltpu.VMEM((length // WIDE, 2 * half, WIDE), BF16),
+            pltpu.VMEM((places[2][1], WIDE), BF16),
+            pltpu.VMEM((places[3][1], WIDE), BF16),
+            pltpu.VMEM((places[4][1], WIDE), BF16),
+            pltpu.VMEM((places[1][1], WIDE), BF16),
             pltpu.SMEM((rows, cols), jnp.int32),
             pltpu.VMEM((2, length, breadth), BF16),
             pltpu.VMEM((2, length, breadth), BF16),
@@ -339,7 +390,7 @@
             pltpu.VMEM((2, breadth, breadth), BF16),
             pltpu.VMEM((2, breadth, breadth), BF16),
             pltpu.VMEM((8, breadth, breadth), F32),
-            dma((chunks,)),
+            dma((length // WIDE,)),
             dma((5,)),
             dma((2,)),
             dma((4,)),
@@ -352,12 +403,9 @@
             dma((8,)),
         ],
         compiler_params=pltpu.CompilerParams(
-            collective_id=0, has_side_effects=True, vmem_limit_bytes=40 * 1024 * 1024
+            collective_id=0, has_side_effects=True, vmem_limit_bytes=54500 * 1024
         ),
-    )(
-        strips.reshape(4, length, breadth), occupancy, table, inverse, corner_table,
-        corner_inverse, spins,
-    )
+    )(strips.reshape(4, length, breadth), occupancy, tables)
     return result[None, None]
 
 

time: 61.2 us -> 37.2 us (0.61)
  Pallas kernels: 50.2 us -> 35.2 us
  local copies, waits for them, and re-layouts: 10.1 us -> 1.49 us
    pallas_call x1, Pallas kernels: 50.2 us -> 35.2 us  [per_device(): pl.pallas_call(functools.partial(kernel, rows, cols, length, breadth), ou...]
    unnamed x15 -> x3, local copies, waits for them, and re-layouts: 10.1 us -> 1.49 us
where the time goes in v2:
time: 37.2 us; the launch traced here: 36.7 us
  Pallas kernels  35.2 us (95%)
  local copies, waits for them, and re-layouts  1.49 us (4%)
    pallas_call x1, Pallas kernels, per_device(): pl.pallas_call(functools.partial(kernel, rows, cols, length, breadth), ou...  35.2 us
    unnamed x3, local copies, waits for them, and re-layouts  1.49 us

profile of v2, /device:TPU:1, one launch (start us, length us, event | category | flops | bytes accessed | tf_op | source)
XLA Modules:
  0.0 36.7 jit_solution(4007787431936509281)
XLA Ops:
  0.0 0.0 copy-start
  0.0 0.7 %copy-done = s32[16,16]{1,0:T(8,128)S(1)} copy-done((s32[16,16]{1,0:T(8,128)S(1)}, s32[16,16]{1,0:T(8,128)}, u32[]{:S(2)}) %copy-start) | copy-done | bytes 1048
  0.7 35.2 %shard_map.37 = f32[8,128,128]{2,1,0:T(8,128)S(1)} custom-call(bf16[4,2048,128]{2,1,0:T(8,128)(2,1)} %bitcast.3, s32[16,16]{1,0:T(8,128)S(1)} %copy-done, bf16[18592,256]{1,0:T(8,128)(2,1)} %constant.2.clone.tables), custom_call_target="tpu_custom_call" | custom-call | tf_op jit(solution)/shard_map/pallas_call | solution.py:369
  35.9 0.8 %copy.5 = f32[1,1,8,128,128]{4,3,2,1,0:T(8,128)} copy(f32[1,1,8,128,128]{4,3,2,1,0:T(8,128)S(1)} %bitcast.2) | data formatting | bytes 1048576
Async XLA Ops:
  0.0 0.7 %copy-start = (s32[16,16]{1,0:T(8,128)S(1)}, s32[16,16]{1,0:T(8,128)}, u32[]{:S(2)}) copy-start(s32[16,16]{1,0:T(8,128)} %occ.1) | copy-start | bytes 3076

commit v3 on v2

--- a/solution.py
+++ b/solution.py
@@ -78,11 +78,17 @@
     return np.concatenate([blocks(part) for part in parts], 0)
 
 
+def in_order(q, chunks):
+    if isinstance(q, int):
+        return (0, chunks - 1, *range(1, chunks - 1))[q]
+    return jnp.where(q == 0, 0, jnp.where(q == 1, chunks - 1, q - 1))
+
+
 def kernel(
     rows, cols, length, breadth,
     strips, occ, tables, out,
     tab, inv_tab, ctab, cinv_tab, spin_v, occ_s, own, got, corner_own, corner_got,
-    acc, g_re, g_im, g_inv, z_all, map_out, map_in, out_v,
+    acc, g_re, g_im, g_inv, z_all, out_v,
     tab_sem, small_sem, own_sem, corner_sem, send_sem, recv_sem,
     csend_sem, crecv_sem, msend_sem, mrecv_sem, out_sem,
 ):
@@ -95,13 +101,15 @@
     up, down = lax.rem(row + rows - 1, rows), lax.rem(row + 1, rows)
     left, right = lax.rem(col + cols - 1, cols), lax.rem(col + 1, cols)
 
+    even, odd = parity == 0, parity == 1
+    side = jnp.where(even, left, right)
+    other_side = jnp.where(even, right, left)
     barrier = pltpu.get_barrier_semaphore()
     neighbours = [
-        (up, left), (up, col), (up, right), (row, left),
-        (row, right), (down, left), (down, col), (down, right),
-    ]
-    for neighbour in neighbours:
-        pl.semaphore_signal(barrier, inc=1, device_id=neighbour, device_id_type=MESH)
+        (row, left), (row, right), (up, col), (down, col), (up, other_side), (down, other_side),
+    ]
+    for device in neighbours:
+        pl.semaphore_signal(barrier, inc=1, device_id=device, device_id_type=MESH)
 
     places = table_places(length, breadth)
     small = [
@@ -127,15 +135,14 @@
             tables.at[pl.ds(at, 2 * half)], tab.at[c], tab_sem.at[c]
         )
 
-    for copy in small + corner_loads + own_loads:
-        copy.start()
-    for c in range(length // WIDE):
-        table_load(c).start()
+    def start_loads():
+        for copy in own_loads[::-1] + small[2:] + small[:2] + corner_loads:
+            copy.start()
+        for q in range(length // WIDE):
+            c = in_order(q // (CHUNK // WIDE), chunks) * (CHUNK // WIDE) + q % (CHUNK // WIDE)
+            table_load(c).start()
 
     pl.semaphore_wait(barrier, len(neighbours))
-
-    side = jnp.where(parity == 0, left, right)
-    other_side = jnp.where(parity == 0, right, left)
 
     def strip_copy(idx, c):
         piece = pl.ds(c * CHUNK if isinstance(c, int) else pl.multiple_of(c * CHUNK, CHUNK), CHUNK)
@@ -151,31 +158,45 @@
         )
 
     def corner_copy(k):
-        target = [(down, right), (down, left), (up, left), (up, right)][k]
-        s, place = corner_places[k]
+        if k < 2:
+            source = strips.at[parity, (low, top)[k]]
+            target = ((down, up)[k], other_side)
+            slot = (2 + parity, 1 - parity)[k]
+        else:
+            source = got.at[1, (top, low)[k - 2]]
+            target = ((up, down)[k - 2], col)
+            slot = (parity, 3 - parity)[k - 2]
         return pltpu.make_async_remote_copy(
-            src_ref=strips.at[s, place],
-            dst_ref=corner_got.at[(k + 2) % 4],
+            src_ref=source,
+            dst_ref=corner_got.at[slot],
             send_sem=csend_sem.at[k],
-            recv_sem=crecv_sem.at[(k + 2) % 4],
+            recv_sem=crecv_sem.at[slot],
             device_id=target,
             device_id_type=MESH,
         )
 
-    for k in range(4):
-        corner_copy(k).start()
+    def corner_wait(slot):
+        pltpu.make_async_remote_copy(
+            src_ref=corner_own.at[slot],
+            dst_ref=corner_got.at[slot],
+            send_sem=csend_sem.at[0],
+            recv_sem=crecv_sem.at[slot],
+            device_id=(row, left),
+            device_id_type=MESH,
+        ).wait_recv()
+
     def send(idx):
-        def start(c, carry):
-            strip_copy(idx, c).start()
-            return carry
-
-        lax.fori_loop(0, chunks, start, 0)
+        for q in range(chunks):
+            strip_copy(idx, in_order(q, chunks)).start()
+
+    def send_corners():
+        corner_copy(0).start()
+        corner_copy(1).start()
 
     send(1)
-
-    @pl.when(parity == 1)
-    def _():
-        send(0)
+    send_corners()
+    pl.when(odd)(lambda: send(0))
+    start_loads()
 
     for copy in small:
         copy.wait()
@@ -243,9 +264,14 @@
             z_all[pl.ds(half + at, block), :] = z[:, breadth:]
         return jnp.dot(inv, z_all[...], preferred_element_type=F32)
 
-    def length_step(idx, c, first):
+    def length_step(idx, q, first):
+        c = in_order(q, chunks)
         piece = pl.ds(c * CHUNK if isinstance(c, int) else pl.multiple_of(c * CHUNK, CHUNK), CHUNK)
-        strip_copy(idx, c).wait_recv()
+
+        @pl.when((idx == 0) | (q > 1))
+        def _():
+            strip_copy(idx, c).wait_recv()
+
         x = jnp.concatenate([own[idx, piece, :], got[idx, piece, :]], 1)
         step = jnp.concatenate(
             [tab[c * (CHUNK // WIDE) + k] for k in range(CHUNK // WIDE)], 1
@@ -261,7 +287,7 @@
         steps = [(1, 1), (1, -1), (-1, -1), (-1, 1)]
         for k in range(4):
             corner_loads[k].wait()
-            corner_copy((k + 2) % 4).wait_recv()
+            corner_wait(k)
         x = jnp.concatenate(
             [part for k in range(4) for part in (corner_own[k], corner_got[k])], 1
         )
@@ -275,19 +301,24 @@
         maps = jnp.dot(cinv_tab[:, : 2 * chalf], jnp.concatenate(parts, 1), preferred_element_type=F32)
         for k in range(4):
             slot = (2, 3, 6, 7)[k]
-            out_v[slot] = maps[:, breadth * k : breadth * (k + 1)] * (
-                alive(row, col, *steps[k]) * scale
-            )
+            out_v[slot] = (
+                maps[:, breadth * k : breadth * (k + 1)] * (alive(row, col, *steps[k]) * scale)
+            ).astype(BF16)
             out_copy(slot).start()
 
     def out_copy(slot):
         return pltpu.make_async_copy(out_v.at[slot], out.at[slot], out_sem.at[slot])
 
+    def map_slots(idx):
+        own_slot = jnp.where(idx == 0, 1, 4 * parity)
+        return own_slot, jnp.where(idx == 0, 5, 4 - own_slot)
+
     def map_copy(idx):
         target = (jnp.where(idx == 0, down, row), jnp.where(idx == 0, col, other_side))
+        own_slot, far_slot = map_slots(idx)
         return pltpu.make_async_remote_copy(
-            src_ref=map_out.at[idx],
-            dst_ref=map_in.at[idx],
+            src_ref=out_v.at[own_slot],
+            dst_ref=out.at[far_slot],
             send_sem=msend_sem.at[idx],
             recv_sem=mrecv_sem.at[idx],
             device_id=target,
@@ -297,14 +328,19 @@
     for copy in own_loads:
         copy.wait()
 
-    corners()
-
-    @pl.when(parity == 0)
-    def _():
-        send(0)
+    def hand_on():
+        strip_copy(1, 0).wait_recv()
+        corner_copy(2).start()
+        strip_copy(1, chunks - 1).wait_recv()
+        corner_copy(3).start()
+
+    corner_phase = 1
+    corner_step = chunks
 
     def phase(p, carry):
         idx = lax.rem(p + parity, 2)
+
+        pl.when(idx == 1)(hand_on)
 
         @pl.when(p == 0)
         def _():
@@ -313,13 +349,19 @@
 
         length_step(idx, 0, True)
 
-        def more(c, inner):
+
+        def more(q, inner):
             @pl.when(p == 0)
             def _():
                 for k in range(CHUNK // WIDE):
-                    table_load(c * (CHUNK // WIDE) + k).wait()
-
-            length_step(idx, c, False)
+                    table_load(in_order(q, chunks) * (CHUNK // WIDE) + k).wait()
+
+            @pl.when((p == corner_phase) & (q == corner_step))
+            def _():
+                corners()
+
+            length_step(idx, q, False)
+            pl.when((p == 0) & even & (q == 1))(lambda: send(0))
             return inner
 
         lax.fori_loop(1, chunks, more, 0)
@@ -329,23 +371,17 @@
             row, col, jnp.where(idx == 0, 1, 0), jnp.where(idx == 0, 0, 1 - 2 * parity)
         )
         result = result * (live * (1.0 / math.sqrt(length * breadth)))
-        map_out[idx] = result.astype(BF16)
+        slot, _ = map_slots(idx)
+        out_v[slot] = result.astype(BF16)
         map_copy(idx).start()
-        slot = jnp.where(idx == 0, 1, 4 * parity)
-        out_v[slot] = result
         out_copy(slot).start()
         return carry
 
     lax.fori_loop(0, 2, phase, 0)
+    corners()
 
     for idx in (1, 0):
-        map_copy(idx).wait_recv()
-        slot = 4 * (1 - parity) if idx == 1 else 5
-        out_v[slot] = map_in[idx].astype(F32)
-        out_copy(slot).start()
-
-    for idx in (1, 0):
-        map_copy(idx).wait_send()
+        map_copy(idx).wait()
 
         def sent(c, carry, idx=idx):
             strip_copy(idx, c).wait_send()
@@ -354,7 +390,7 @@
         lax.fori_loop(0, chunks, sent, 0)
     for k in range(4):
         corner_copy(k).wait_send()
-    for slot in range(8):
+    for slot in (2, 3, 6, 7, 1, 4 * parity):
         out_copy(slot).wait()
 
 
@@ -368,7 +404,7 @@
     dma = pltpu.SemaphoreType.DMA
     result = pl.pallas_call(
         functools.partial(kernel, rows, cols, length, breadth),
-        out_shape=jax.ShapeDtypeStruct((8, breadth, breadth), F32),
+        out_shape=jax.ShapeDtypeStruct((8, breadth, breadth), BF16),
         in_specs=[hbm] * 3,
         out_specs=hbm,
         scratch_shapes=[
@@ -387,9 +423,7 @@
             pltpu.VMEM((half, breadth), F32),
             pltpu.VMEM((half, breadth), F32),
             pltpu.VMEM((2 * half, breadth), BF16),
-            pltpu.VMEM((2, breadth, breadth), BF16),
-            pltpu.VMEM((2, breadth, breadth), BF16),
-            pltpu.VMEM((8, breadth, breadth), F32),
+            pltpu.VMEM((8, breadth, breadth), BF16),
             dma((length // WIDE,)),
             dma((5,)),
             dma((2,)),
@@ -406,7 +440,7 @@
             collective_id=0, has_side_effects=True, vmem_limit_bytes=54500 * 1024
         ),
     )(strips.reshape(4, length, breadth), occupancy, tables)
-    return result[None, None]
+    return result.astype(F32)[None, None]
 
 
 def solution(mesh):

time: 37.2 us -> 37 us (level)
  other arithmetic: 0 us -> 0.83 us
  local copies, waits for them, and re-layouts: 1.49 us -> 0.7 us
    broadcast_in_dim x0 -> x1, other arithmetic: none -> 0.83 us  [per_device(): return result.astype(F32)[None, None]]
    unnamed x3 -> x2, local copies, waits for them, and re-layouts: 1.49 us -> 0.7 us
where the time goes in v3:
time: 37 us; the launch traced here: 36.9 us
  Pallas kernels  35.3 us (95%)
  other arithmetic  0.83 us (2%)
  local copies, waits for them, and re-layouts  0.7 us (2%)
    pallas_call x1, Pallas kernels, per_device(): pl.pallas_call(functools.partial(kernel, rows, cols, length, breadth), ou...  35.3 us
    broadcast_in_dim x1, other arithmetic, per_device(): return result.astype(F32)[None, None]  0.83 us

profile of v3, /device:TPU:1, one launch (start us, length us, event | category | flops | bytes accessed | tf_op | source)
XLA Modules:
  0.0 36.9 jit_solution(729319934693776972)
XLA Ops:
  0.0 0.0 copy-start
  0.0 0.7 %copy-done = s32[16,16]{1,0:T(8,128)S(1)} copy-done((s32[16,16]{1,0:T(8,128)S(1)}, s32[16,16]{1,0:T(8,128)}, u32[]{:S(2)}) %copy-start) | copy-done | bytes 1048
  0.7 35.3 %shard_map.37 = bf16[8,128,128]{2,1,0:T(8,128)(2,1)S(1)} custom-call(bf16[4,2048,128]{2,1,0:T(8,128)(2,1)} %bitcast.4, s32[16,16]{1,0:T(8,128)S(1)} %copy-done, bf16[18592,256]{1,0:T(8,128)(2,1)} %constant.2.clone.tables), custom_call_target="tpu_custom_call" | custom-call | tf_op jit(solution)/shard_map/pallas_call | solution.py:405
  36.0 0.8 %bitcast_convert_fusion = f32[1,1,8,128,128]{4,3,2,1,0:T(8,128)} fusion(bf16[8,128,128]{2,1,0:T(8,128)(2,1)S(1)} %shard_map.37), kind=kLoop, calls=%fused_computation | loop fusion | flops 131072 | bytes 786432 | tf_op jit(solution)/shard_map/broadcast_in_dim | solution.py:443
Async XLA Ops:
  0.0 0.7 %copy-start = (s32[16,16]{1,0:T(8,128)S(1)}, s32[16,16]{1,0:T(8,128)}, u32[]{:S(2)}) copy-start(s32[16,16]{1,0:T(8,128)} %occ.1) | copy-start | bytes 3076

commit v4 on v3

--- a/solution.py
+++ b/solution.py
@@ -136,7 +136,7 @@
         )
 
     def start_loads():
-        for copy in own_loads[::-1] + small[2:] + small[:2] + corner_loads:
+        for copy in own_loads[::-1] + small:
             copy.start()
         for q in range(length // WIDE):
             c = in_order(q // (CHUNK // WIDE), chunks) * (CHUNK // WIDE) + q % (CHUNK // WIDE)
@@ -185,8 +185,8 @@
             device_id_type=MESH,
         ).wait_recv()
 
-    def send(idx):
-        for q in range(chunks):
+    def send(idx, numbers=None):
+        for q in range(chunks) if numbers is None else numbers:
             strip_copy(idx, in_order(q, chunks)).start()
 
     def send_corners():
@@ -361,10 +361,16 @@
                 corners()
 
             length_step(idx, q, False)
-            pl.when((p == 0) & even & (q == 1))(lambda: send(0))
+            pl.when((p == 0) & even & (q == 1))(lambda: send(0, (0, 1)))
+            pl.when((p == 0) & even & (q == 3))(lambda: send(0, (2, 3)))
             return inner
 
         lax.fori_loop(1, chunks, more, 0)
+        @pl.when(p == 0)
+        def _():
+            for copy in corner_loads:
+                copy.start()
+
         sign = jnp.where(idx == 0, 1, 1 - 2 * parity).astype(F32)
         result = edge_map(sign)
         live = alive(

time: 37 us -> 37 us (level)
  no operation moved by 1% of the time
where the time goes in v4:
time: 37 us; the launch traced here: 36.9 us
  Pallas kernels  35.3 us (95%)
  other arithmetic  0.83 us (2%)
  local copies, waits for them, and re-layouts  0.7 us (2%)
    pallas_call x1, Pallas kernels, per_device(): pl.pallas_call(functools.partial(kernel, rows, cols, length, breadth), ou...  35.3 us
    broadcast_in_dim x1, other arithmetic, per_device(): return result.astype(F32)[None, None]  0.83 us

profile of v4, /device:TPU:1, one launch (start us, length us, event | category | flops | bytes accessed | tf_op | source)
XLA Modules:
  0.0 36.9 jit_solution(4146080107784898047)
XLA Ops:
  0.0 0.0 copy-start
  0.0 0.7 %copy-done = s32[16,16]{1,0:T(8,128)S(1)} copy-done((s32[16,16]{1,0:T(8,128)S(1)}, s32[16,16]{1,0:T(8,128)}, u32[]{:S(2)}) %copy-start) | copy-done | bytes 1048
  0.7 35.3 %shard_map.37 = bf16[8,128,128]{2,1,0:T(8,128)(2,1)S(1)} custom-call(bf16[4,2048,128]{2,1,0:T(8,128)(2,1)} %bitcast.4, s32[16,16]{1,0:T(8,128)S(1)} %copy-done, bf16[18592,256]{1,0:T(8,128)(2,1)} %constant.2.clone.tables), custom_call_target="tpu_custom_call" | custom-call | tf_op jit(solution)/shard_map/pallas_call | solution.py:411
  36.0 0.8 %bitcast_convert_fusion = f32[1,1,8,128,128]{4,3,2,1,0:T(8,128)} fusion(bf16[8,128,128]{2,1,0:T(8,128)(2,1)S(1)} %shard_map.37), kind=kLoop, calls=%fused_computation | loop fusion | flops 131072 | bytes 786432 | tf_op jit(solution)/shard_map/broadcast_in_dim | solution.py:449
Async XLA Ops:
  0.0 0.7 %copy-start = (s32[16,16]{1,0:T(8,128)S(1)}, s32[16,16]{1,0:T(8,128)}, u32[]{:S(2)}) copy-start(s32[16,16]{1,0:T(8,128)} %occ.1) | copy-start | bytes 3076

commit v5 on v3

--- a/solution.py
+++ b/solution.py
@@ -361,7 +361,7 @@
                 corners()
 
             length_step(idx, q, False)
-            pl.when((p == 0) & even & (q == 1))(lambda: send(0))
+            pl.when((p == 0) & even & (q == 1 + lax.rem(row // 2, 2)))(lambda: send(0))
             return inner
 
         lax.fori_loop(1, chunks, more, 0)

time: 37 us -> 37 us (level)
  no operation moved by 1% of the time
where the time goes in v5:
time: 37 us; the launch traced here: 36.9 us
  Pallas kernels  35.3 us (95%)
  other arithmetic  0.83 us (2%)
  local copies, waits for them, and re-layouts  0.7 us (2%)
    pallas_call x1, Pallas kernels, per_device(): pl.pallas_call(functools.partial(kernel, rows, cols, length, breadth), ou...  35.3 us
    broadcast_in_dim x1, other arithmetic, per_device(): return result.astype(F32)[None, None]  0.83 us

profile of v5, /device:TPU:1, one launch (start us, length us, event | category | flops | bytes accessed | tf_op | source)
XLA Modules:
  0.0 36.9 jit_solution(18195980267973536280)
XLA Ops:
  0.0 0.0 copy-start
  0.0 0.7 %copy-done = s32[16,16]{1,0:T(8,128)S(1)} copy-done((s32[16,16]{1,0:T(8,128)S(1)}, s32[16,16]{1,0:T(8,128)}, u32[]{:S(2)}) %copy-start) | copy-done | bytes 1048
  0.7 35.3 %shard_map.37 = bf16[8,128,128]{2,1,0:T(8,128)(2,1)S(1)} custom-call(bf16[4,2048,128]{2,1,0:T(8,128)(2,1)} %bitcast.4, s32[16,16]{1,0:T(8,128)S(1)} %copy-done, bf16[18592,256]{1,0:T(8,128)(2,1)} %constant.2.clone.tables), custom_call_target="tpu_custom_call" | custom-call | tf_op jit(solution)/shard_map/pallas_call | solution.py:405
  36.0 0.8 %bitcast_convert_fusion = f32[1,1,8,128,128]{4,3,2,1,0:T(8,128)} fusion(bf16[8,128,128]{2,1,0:T(8,128)(2,1)S(1)} %shard_map.37), kind=kLoop, calls=%fused_computation | loop fusion | flops 131072 | bytes 786432 | tf_op jit(solution)/shard_map/broadcast_in_dim | solution.py:443
Async XLA Ops:
  0.0 0.7 %copy-start = (s32[16,16]{1,0:T(8,128)S(1)}, s32[16,16]{1,0:T(8,128)}, u32[]{:S(2)}) copy-start(s32[16,16]{1,0:T(8,128)} %occ.1) | copy-start | bytes 3076
